TPU v7x, 256 devices: a whole 4x4x8 slice. The times are simulated.
256 devices in a mesh: ctx: 8 (over x_lo, y), exp: 32 (over z, x_hi, core).
Axes of the slice: x: 4 (x_hi: 2, x_lo: 2; x = x_hi * 2 + x_lo), y: 4, z: 8, core: 2. Of those that a mesh axis runs over, the one named last changes fastest.
Arguments:
- hidden_in: bfloat16 [32, 1024, 2048], P('exp', 'ctx'), may hold values from -3 to 3
- query: bfloat16 [32, 1024, 4096], P('exp', 'ctx'), may hold values from -96 to 96
- keyval: bfloat16 [32, 1024, 512], P('exp', 'ctx'), may hold values from -5 to 5
- out_proj: bfloat16 [4096, 2048], P('exp'), may hold values from -0.375 to 0.375
- norm_gain: bfloat16 [2048], replicated, may hold values from 0.099609375 to 1.8984375
- expert_ids: int32 [32, 1024, 8], P('exp', 'ctx'), may hold values from 0 to 31, all different within a row; in each aligned block of 128 rows (0 to 127, 128 to 255, ..., all dimensions but the last counted through in order) at most 34 rows name the same one
- gate_weights: float32 [32, 1024, 8], P('exp', 'ctx'), may hold values from 0.1 to 0.4
- w_gate: bfloat16 [32, 2048, 768], P('exp'), may hold values from -0.125 to 0.125
- w_up: bfloat16 [32, 2048, 768], P('exp'), may hold values from -0.125 to 0.125
- w_down: bfloat16 [32, 768, 2048], P('exp'), may hold values from -0.21875 to 0.21875
Outputs:
- layer_out: bfloat16 [32, 1024, 2048], P('exp', 'ctx')
Inputs may be any that keep to these rules, and one draw needn't show every extreme that they name: `expert_ids`: in each aligned block of 128 tokens (the tokens of one device) no expert is named by more than 34 tokens, a bound that some block reaches; a token names 8 different experts.
All inputs are finite; a program needn't handle non-finite values.
Results may differ from a plain program's by a relative error of at most 0.014.
Values may be sent and summed in bfloat16 or wider, within the bound.
A program may use at most 128 MiB of HBM per device.

v0:
```python
import jax
import jax.numpy as jnp
from jax import lax
from jax.sharding import PartitionSpec as P

D = 2048
QH = 32
KVH = 2
HD = 128
TOP = 8


def shifted(block, axis, distance):
    devices = range(lax.axis_size(axis))
    route = [(i - distance, i) for i in devices if i - distance in devices]
    return lax.ppermute(block, axis, route)


def absorb(state, queries, kv_block, source, position):
    tok_rows = queries.shape[0]
    group_size = QH // KVH

    def compute(running):
        run_max, run_sum, run_out = running
        key_rows = kv_block[:, : KVH * HD].reshape(tok_rows, KVH, HD)
        values = kv_block[:, KVH * HD :].reshape(tok_rows, KVH, HD)
        grouped = queries.reshape(tok_rows, KVH, group_size, HD)
        scores = jnp.einsum(
            "qhgd,khd->hgqk", grouped, key_rows, preferred_element_type=jnp.float32
        ) * HD ** (-0.5)
        offsets = jnp.arange(tok_rows, dtype=jnp.int32)
        visible = (position * tok_rows + offsets)[:, None] >= (source * tok_rows + offsets)[None, :]
        scores = jnp.where(visible, scores, -1e30)
        new_max = jnp.maximum(run_max, jnp.max(scores, axis=-1))
        weights = jnp.where(visible, jnp.exp(scores - new_max[..., None]), 0.0)
        rescale = jnp.exp(run_max - new_max)
        run_sum = run_sum * rescale + jnp.sum(weights, axis=-1)
        mixed = jnp.einsum(
            "hgqk,khd->hgqd",
            weights.astype(jnp.bfloat16),
            values,
            preferred_element_type=jnp.float32,
        )
        run_out = run_out * rescale[..., None] + mixed
        return (new_max, run_sum, run_out)

    return lax.cond(source > position, lambda running: running, compute, state)


def body(
    hidden_in, query, keyval, out_proj, norm_gain, expert_ids, gate_weights, w_gate, w_up, w_down
):
    n_ctx = lax.axis_size("ctx")
    n_exp = lax.axis_size("exp")
    position = lax.axis_index("ctx")
    tok_rows = hidden_in.shape[1]
    group_size = QH // KVH
    queries = query[0]
    local_kv = keyval[0]
    state = (
        jnp.full((KVH, group_size, tok_rows), -1e30, jnp.float32),
        jnp.zeros((KVH, group_size, tok_rows), jnp.float32),
        jnp.zeros((KVH, group_size, tok_rows, HD), jnp.float32),
    )
    current = local_kv
    for pass_step in range(n_ctx):
        source = (position - pass_step) % n_ctx
        state = absorb(state, queries, current, source, position)
        if pass_step + 1 < n_ctx:
            current = shifted(current, "ctx", 1)
    run_max, run_sum, run_out = state
    attended = (
        (run_out / run_sum[..., None])
        .transpose(2, 0, 1, 3)
        .reshape(tok_rows, QH * HD)
        .astype(jnp.bfloat16)
    )
    projected = jnp.dot(
        attended,
        lax.all_gather(out_proj, "exp", axis=0, tiled=True),
        preferred_element_type=jnp.float32,
    )
    residual = hidden_in[0].astype(jnp.float32) + projected
    scale_inv = lax.rsqrt(jnp.mean(residual * residual, axis=-1, keepdims=True) + 1e-06)
    normed = (residual * scale_inv * norm_gain.astype(jnp.float32)).astype(jnp.bfloat16)
    local_experts = w_gate.shape[0]
    experts_all = n_exp * local_experts
    capacity = min(tok_rows, tok_rows * TOP // experts_all + tok_rows * TOP // (16 * experts_all))
    routes = expert_ids[0].reshape(-1)
    onehot = (routes[:, None] == jnp.arange(experts_all, dtype=jnp.int32)[None, :]).astype(
        jnp.int32
    )
    slot_rank = jnp.sum(onehot * (jnp.cumsum(onehot, axis=0) - 1), axis=1)
    target = routes * capacity + slot_rank
    send_rows = (
        jnp.zeros((experts_all * capacity, D), jnp.bfloat16)
        .at[target]
        .set(jnp.repeat(normed, TOP, axis=0))
    )
    send_rows = send_rows.reshape(experts_all, capacity, D)
    arrived = lax.all_to_all(send_rows, "exp", split_axis=0, concat_axis=0, tiled=True)
    slots = arrived.shape[1]
    grouped = arrived.reshape(n_exp, local_experts, slots, D)
    gate_pre = jnp.einsum("sxcd,xdf->sxcf", grouped, w_gate, preferred_element_type=jnp.float32)
    up_pre = jnp.einsum("sxcd,xdf->sxcf", grouped, w_up, preferred_element_type=jnp.float32)
    activated = (jax.nn.silu(gate_pre) * up_pre).astype(jnp.bfloat16)
    expert_out = jnp.einsum(
        "sxcf,xfd->sxcd", activated, w_down, preferred_element_type=jnp.float32
    ).astype(jnp.bfloat16)
    returned = lax.all_to_all(
        expert_out.reshape(n_exp * local_experts, slots, D),
        "exp",
        split_axis=0,
        concat_axis=0,
        tiled=True,
    )
    picked = returned.reshape(experts_all * capacity, D)[target].reshape(tok_rows, TOP, D)
    expert_sum = jnp.sum(gate_weights[0][..., None] * picked.astype(jnp.float32), axis=1)
    result = (residual + expert_sum).astype(jnp.bfloat16)
    return result[None]


def solution(mesh):
    in_specs = (
        P("exp", "ctx", None),
        P("exp", "ctx", None),
        P("exp", "ctx", None),
        P("exp", None),
        P(),
        P("exp", "ctx", None),
        P("exp", "ctx", None),
        P("exp", None, None),
        P("exp", None, None),
        P("exp", None, None),
    )
    out_specs = P("exp", "ctx", None)
    return jax.shard_map(body, mesh=mesh, in_specs=in_specs, out_specs=out_specs, check_vma=False)
```

profile of v0, /device:TPU:25, one launch (start us, length us, event | category | flops | bytes accessed | tf_op | source)
XLA Modules:
  0.0 491.0 jit_solution(2092161463114498345)
XLA Ops:
  7.3 1.1 copy.60
  8.4 2.8 collective-permute-start
  11.2 3.5 collective-permute-done
  14.7 4.9 collective-permute-start.1
  19.6 1.9 collective-permute-done.1
  21.5 5.9 %collective-permute-start.2 = (bf16[128,512]{0,1:T(8,128)(2,1)S(1)}, bf16[128,512]{0,1:T(8,128)(2,1)}, u32[]{:S(2)}, u32[]{:S(2)}) collective-permute-start(bf16[128,512]{0,1:T(8,128)(2,1)S(1)} %collective-permute-done.1), channel_id=1, source_target_pairs={{0,32},{32,64},{64,96},{96,128},{128,160},{160,192},{192,224},{1,3... | collective-permute-start | bytes 393224 | tf_op jit(solution)/shard_map/ppermute | solution.py:16
  27.4 0.8 copy.64
  28.3 3.9 collective-permute-done.2
  32.1 6.3 %collective-permute-start.3 = (bf16[128,512]{0,1:T(8,128)(2,1)}, bf16[128,512]{0,1:T(8,128)(2,1)}, u32[]{:S(2)}, u32[]{:S(2)}) collective-permute-start(bf16[128,512]{0,1:T(8,128)(2,1)} %collective-permute-done.2), channel_id=1, source_target_pairs={{0,32},{32,64},{64,96},{96,128},{128,160},{160,192},{192,224},{1,3... | collective-permute-start | bytes 393224 | tf_op jit(solution)/shard_map/ppermute | solution.py:16
  39.1 15.6 %reduce-window.6 = s32[32,8,128]{2,1,0:T(8,128)S(1)} reduce-window(s32[32,8,128]{2,1,0:T(8,128)} %fusion.137, s32[]{:T(128)} %constant.164.clone.1), window={size=1x1x128 pad=0_0x0_0x127_0}, to_apply=%region_32.33 | reduce-window | flops 4161536 | bytes 262148 | tf_op jit(solution)/shard_map/reduce-window
  55.5 1.0 copy.66
  56.6 1.9 collective-permute-start.4
  59.3 3.3 collective-permute-done.4
  62.6 4.0 collective-permute-start.5
  67.8 5.5 %conditional.8 = (f32[2,16,128]{2,1,0:T(8,128)S(1)}, f32[2,16,128]{2,1,0:T(8,128)S(1)}, f32[2,16,128,128]{3,2,1,0:T(8,128)}) conditional(s32[]{:T(128)} %convert_element_type.101, (s32[]{:T(128)}, s32[]{:T(128)}, bf16[128,512]{0,1:T(8,128)(2,1)S(1)}, bf16[1,128,4096]{2,1,0:T(8,128)(2,1)}) %tuple.119, () %tuple.57), branch_computations={%region_0.3_spmd, %region_3.4_spmd} | conditional | flops 275808512 | bytes 12175416 | solution.py:47
  67.9 1.8 copy.126
  71.0 2.3 convolution_add_fusion
  73.3 2.3 collective-permute-start.6
  75.6 7.2 %conditional.9 = (f32[2,16,128]{2,1,0:T(8,128)S(1)}, f32[2,16,128]{2,1,0:T(8,128)S(1)}, f32[2,16,128,128]{3,2,1,0:T(8,128)}) conditional(s32[]{:T(128)} %convert_element_type.100, (s32[]{:T(128)}, s32[]{:T(128)}, bf16[128,512]{0,1:T(8,128)(2,1)}, bf16[1,128,4096]{2,1,0:T(8,128)(2,1)}, f32[2,16,128]{2,1,0:T(8,128)S(1)}, ...), branch_computations={%region_4.7_spmd, %region_7.8_spmd} | conditional | flops 276324608 | bytes 14321720 | solution.py:47
  75.7 0.9 fusion.140
  76.6 1.4 copy.127
  79.3 3.5 multiply_add_fusion
  82.8 6.3 %conditional.10 = (f32[2,16,128]{2,1,0:T(8,128)S(1)}, f32[2,16,128]{2,1,0:T(8,128)S(1)}, f32[2,16,128,128]{3,2,1,0:T(8,128)}) conditional(s32[]{:T(128)} %convert_element_type.99, (s32[]{:T(128)}, s32[]{:T(128)}, bf16[128,512]{0,1:T(8,128)(2,1)S(1)}, bf16[1,128,4096]{2,1,0:T(8,128)(2,1)}, f32[2,16,128]{2,1,0:T(8,128)S(1)}, ...), branch_computations={%region_8.11_spmd, %region_11.12_spmd} | conditional | flops 276324608 | bytes 14321720 | solution.py:47
  82.9 1.4 copy.128
  85.6 3.5 multiply_add_fusion.2
  89.1 7.2 %conditional.11 = (f32[2,16,128]{2,1,0:T(8,128)S(1)}, f32[2,16,128]{2,1,0:T(8,128)S(1)}, f32[2,16,128,128]{3,2,1,0:T(8,128)}) conditional(s32[]{:T(128)} %convert_element_type.98, (s32[]{:T(128)}, s32[]{:T(128)}, bf16[128,512]{0,1:T(8,128)(2,1)}, bf16[1,128,4096]{2,1,0:T(8,128)(2,1)}, f32[2,16,128]{2,1,0:T(8,128)S(1)}, ...), branch_computations={%region_12.15_spmd, %region_15.16_spmd} | conditional | flops 276324608 | bytes 14321720 | solution.py:47
  89.2 0.9 fusion.142
  90.1 1.4 copy.129
  92.8 3.5 multiply_add_fusion.4
  96.6 6.3 %conditional.15 = (f32[2,16,128]{2,1,0:T(8,128)S(1)}, f32[2,16,128,128]{2,3,1,0:T(8,128)}) conditional(s32[]{:T(128)} %convert_element_type.94, (s32[]{:T(128)}, s32[]{:T(128)}, bf16[128,512]{0,1:T(8,128)(2,1)S(1)}, bf16[1,128,4096]{2,1,0:T(8,128)(2,1)}, f32[2,16,128]{2,1,0:T(8,128)S(1)}, /*index=5*/f32[2,16,128]{2,1,0:T(8,128)S(1)}, ...), branch_computations={%region_28.31_spmd, %region_31.32_spmd} | conditional | flops 276324608 | bytes 18516016 | solution.py:47
  96.6 2.9 copy.125
  102.9 2.8 divide_convert_fusion
  105.8 51.9 %all-gather.2.cloned.1.call-done = bf16[4096,2048]{1,0:T(8,128)(2,1)} async-done(((bf16[128,2048]{1,0:T(8,128)(2,1)}), bf16[4096,2048]{1,0:T(8,128)(2,1)}) %all-gather.2.cloned.1.call-update) | async-done | bytes 16777232 | tf_op jit(solution)/shard_map/all_gather | solution.py:80
  157.7 8.5 %multiply_reduce_fusion = (f32[128]{0:T(128)S(1)}, f32[128,2048]{1,0:T(8,128)S(1)}) fusion(bf16[128,4096]{0,1:T(8,128)(2,1)} %bitcast.314, bf16[4096,2048]{1,0:T(8,128)(2,1)} %all-gather.2.cloned.1.call-done, bf16[1,128,2048]{2,1,0:T(8,128)(2,1)} %param.26), kind=kOutput, calls=%fused_computation.195 | convolution fusion | flops 2148532224 | bytes 19399168 | tf_op jit(solution)/shard_map/dot_general | solution.py:78
  166.3 0.9 copy-done.1
  167.2 0.9 multiply_convert_fusion
  168.2 9.7 %scatter_custom_fusion = bf16[1088,2048]{1,0:T(8,128)(2,1)} fusion(s32[1024]{0:T(1024)S(1)} %bitcast.344, bf16[]{:T(256)} %constant.173.clone.1, bf16[128,2048]{1,0:T(8,128)(2,1)} %multiply_convert_fusion), kind=kCustom, calls=%fused_computation.173 | custom fusion | bytes 4980738 | tf_op jit(solution)/shard_map/scatter | solution.py:98
  177.8 7.3 %reshape.231 = bf16[32,34,2048]{2,1,0:T(8,128)(2,1)} reshape(bf16[1088,2048]{1,0:T(8,128)(2,1)} %scatter_custom_fusion) | data formatting | bytes 8912896 | tf_op jit(solution)/shard_map/reshape | solution.py:100
  185.1 123.2 %all_to_all.10 = bf16[32,34,2048]{2,1,0:T(8,128)(2,1)S(1)} all-to-all(bf16[32,34,2048]{2,1,0:T(8,128)(2,1)} %reshape.231), channel_id=1, replica_groups=mesh['ctx'=8,'exp'=32] {'exp'}, dimensions={0} | all-to-all | bytes 8912896 | tf_op jit(solution)/shard_map/all_to_all | solution.py:101
  308.3 2.3 copy-done.3
  310.7 6.4 %fusion.121 = f32[32,34,768]{2,1,0:T(8,128)} fusion(bf16[32,34,2048]{2,1,0:T(8,128)(2,1)S(1)} %all_to_all.10, bf16[1,2048,768]{2,1,0:T(8,128)(2,1)S(1)} %copy-done.10), kind=kOutput, calls=%fused_computation.184 | convolution fusion | flops 3422552064 | bytes 10944512 | tf_op jit(solution)/shard_map/sxcd,xdf->sxcf/dot_general | solution.py:105
  317.1 14.6 %convolution_convert_fusion = bf16[32,34,2048]{2,1,0:T(8,128)(2,1)} fusion(bf16[1,768,2048]{2,1,0:T(8,128)(2,1)S(1)} %copy-done, f32[32,34,768]{2,1,0:T(8,128)} %fusion.121, bf16[32,34,2048]{2,1,0:T(8,128)(2,1)} %copy-done.3, bf16[1,2048,768]{2,1,0:T(8,128)(2,1)} %param.33), kind=kOutput, calls=%fused_computation.175 | convolution fusion | flops 6852345856 | bytes 18546688 | tf_op jit(solution)/shard_map/sxcf,xfd->sxcd/dot_general | solution.py:107
  331.7 6.5 %all-to-all-start.1 = ((bf16[32,34,2048]{2,1,0:T(8,128)(2,1)}), bf16[32,34,2048]{2,1,0:T(8,128)(2,1)}, u32[]{:S(2)}, u32[]{:S(2)}) async-start(bf16[32,34,2048]{2,1,0:T(8,128)(2,1)} %convolution_convert_fusion), calls=%async_computation.1 | async-start | bytes 10485760 | tf_op jit(solution)/shard_map/all_to_all | solution.py:110
  338.3 118.8 %all-to-all-done.1 = bf16[32,34,2048]{2,1,0:T(8,128)(2,1)} async-done(((bf16[32,34,2048]{2,1,0:T(8,128)(2,1)}), bf16[32,34,2048]{2,1,0:T(8,128)(2,1)}, u32[]{:S(2)}, u32[]{:S(2)}) %all-to-all-start.1) | async-done | bytes 4456480 | tf_op jit(solution)/shard_map/all_to_all | solution.py:110
  457.1 7.4 %reshape.236 = bf16[1088,2048]{1,0:T(8,128)(2,1)} reshape(bf16[32,34,2048]{2,1,0:T(8,128)(2,1)} %all-to-all-done.1) | data formatting | bytes 8912896 | tf_op jit(solution)/shard_map/reshape | solution.py:117
  464.5 11.7 %gather_fusion = bf16[1024,2048]{1,0:T(8,128)(2,1)} fusion(bf16[1088,2048]{1,0:T(8,128)(2,1)} %reshape.236, s32[1024]{0:T(1024)S(1)} %broadcast_clamp_fusion), kind=kCustom, calls=%fused_computation | custom fusion | bytes 8392704 | tf_op jit(solution)/shard_map/gather | solution.py:117
  476.2 6.6 %fusion.113 = f32[128,2048]{1,0:T(8,128)S(1)} fusion(bf16[1024,2048]{1,0:T(8,128)(2,1)} %gather_fusion, f32[128,8]{1,0:T(8,128)S(1)} %copy.62), kind=kLoop, calls=%fused_computation.172 | loop fusion | flops 6029312 | bytes 5246976 | tf_op jit(solution)/shard_map/reduce_sum | solution.py:118
  482.8 0.9 fusion.134
  (74 shorter events, 9.9 us)
Async XLA Ops:
  6.5 310.6 %copy-start = (bf16[1,768,2048]{2,1,0:T(8,128)(2,1)S(1)}, bf16[1,768,2048]{2,1,0:T(8,128)(2,1)}, u32[]{:S(2)}) copy-start(bf16[1,768,2048]{2,1,0:T(8,128)(2,1)} %param.35) | copy-start | bytes 9437188
  6.5 61.0 %copy-start.8 = (bf16[2048]{0:T(1024)(128)(2,1)S(1)}, bf16[2048]{0:T(1024)(128)(2,1)}, u32[]{:S(2)}) copy-start(bf16[2048]{0:T(1024)(128)(2,1)} %param.30) | copy-start | bytes 12292
  6.5 151.2 %all-gather.2.cloned.1.call-start = ((), (), s32[]{:S(2)}) async-start(), calls=%async_computation.2 | async-start | bytes 17301504 | tf_op jit(solution)/shard_map/all_gather | solution.py:80
  8.4 6.3 %collective-permute-start = (bf16[128,512]{0,1:T(8,128)(2,1)S(1)}, bf16[128,512]{0,1:T(8,128)(2,1)S(1)}, u32[]{:S(2)}, u32[]{:S(2)}) collective-permute-start(bf16[128,512]{0,1:T(8,128)(2,1)S(1)} %bitcast.323), channel_id=1, source_target_pairs={{0,32},{32,64},{64,96},{96,128},{128,160},{160,192},{192,224},{1,3... | collective-permute-start | bytes 393224 | tf_op jit(solution)/shard_map/ppermute | solution.py:16
  14.7 6.8 %copy-start.7 = (bf16[128,512]{0,1:T(8,128)(2,1)}, bf16[128,512]{0,1:T(8,128)(2,1)S(1)}, u32[]{:S(2)}) copy-start(bf16[128,512]{0,1:T(8,128)(2,1)S(1)} %collective-permute-done) | copy-start | bytes 393220
  14.7 6.8 %collective-permute-start.1 = (bf16[128,512]{0,1:T(8,128)(2,1)S(1)}, bf16[128,512]{0,1:T(8,128)(2,1)S(1)}, u32[]{:S(2)}, u32[]{:S(2)}) collective-permute-start(bf16[128,512]{0,1:T(8,128)(2,1)S(1)} %collective-permute-done), channel_id=1, source_target_pairs={{0,32},{32,64},{64,96},{96,128},{128,160},{160,192},{192,224},{1,3... | collective-permute-start | bytes 393224 | tf_op jit(solution)/shard_map/ppermute | solution.py:16
  21.5 17.0 %copy-start.5 = (bf16[128,512]{0,1:T(8,128)(2,1)}, bf16[128,512]{0,1:T(8,128)(2,1)S(1)}, u32[]{:S(2)}) copy-start(bf16[128,512]{0,1:T(8,128)(2,1)S(1)} %collective-permute-done.1) | copy-start | bytes 393220
  21.5 10.7 %collective-permute-start.2 = (bf16[128,512]{0,1:T(8,128)(2,1)S(1)}, bf16[128,512]{0,1:T(8,128)(2,1)}, u32[]{:S(2)}, u32[]{:S(2)}) collective-permute-start(bf16[128,512]{0,1:T(8,128)(2,1)S(1)} %collective-permute-done.1), channel_id=1, source_target_pairs={{0,32},{32,64},{64,96},{96,128},{128,160},{160,192},{192,224},{1,3... | collective-permute-start | bytes 393224 | tf_op jit(solution)/shard_map/ppermute | solution.py:16
  32.1 24.5 %collective-permute-start.3 = (bf16[128,512]{0,1:T(8,128)(2,1)}, bf16[128,512]{0,1:T(8,128)(2,1)}, u32[]{:S(2)}, u32[]{:S(2)}) collective-permute-start(bf16[128,512]{0,1:T(8,128)(2,1)} %collective-permute-done.2), channel_id=1, source_target_pairs={{0,32},{32,64},{64,96},{96,128},{128,160},{160,192},{192,224},{1,3... | collective-permute-start | bytes 393224 | tf_op jit(solution)/shard_map/ppermute | solution.py:16
  56.6 6.0 %collective-permute-start.4 = (bf16[128,512]{0,1:T(8,128)(2,1)}, bf16[128,512]{0,1:T(8,128)(2,1)}, u32[]{:S(2)}, u32[]{:S(2)}) collective-permute-start(bf16[128,512]{0,1:T(8,128)(2,1)} %collective-permute-done.3), channel_id=1, source_target_pairs={{0,32},{32,64},{64,96},{96,128},{128,160},{160,192},{192,224},{1,3... | collective-permute-start | bytes 393224 | tf_op jit(solution)/shard_map/ppermute | solution.py:16
  62.6 10.6 %collective-permute-start.5 = (bf16[128,512]{0,1:T(8,128)(2,1)}, bf16[128,512]{0,1:T(8,128)(2,1)}, u32[]{:S(2)}, u32[]{:S(2)}) collective-permute-start(bf16[128,512]{0,1:T(8,128)(2,1)} %collective-permute-done.4), channel_id=1, source_target_pairs={{0,32},{32,64},{64,96},{96,128},{128,160},{160,192},{192,224},{1,3... | collective-permute-start | bytes 393224 | tf_op jit(solution)/shard_map/ppermute | solution.py:16
  67.8 5.5 %copy-start.4 = (s32[32,8,128]{2,1,0:T(8,128)S(1)}, s32[32,8,128]{2,1,0:T(8,128)}, u32[]{:S(2)}) copy-start(s32[32,8,128]{2,1,0:T(8,128)} %add_add_fusion) | copy-start | bytes 393220
  73.3 23.3 %collective-permute-start.6 = (bf16[128,512]{0,1:T(8,128)(2,1)}, bf16[128,512]{0,1:T(8,128)(2,1)S(1)}, u32[]{:S(2)}, u32[]{:S(2)}) collective-permute-start(bf16[128,512]{0,1:T(8,128)(2,1)} %collective-permute-done.5), channel_id=1, source_target_pairs={{0,32},{32,64},{64,96},{96,128},{128,160},{160,192},{192,224},{1,3... | collective-permute-start | bytes 393224 | tf_op jit(solution)/shard_map/ppermute | solution.py:16
  75.6 7.2 %copy-start.6 = (bf16[128,512]{0,1:T(8,128)(2,1)S(1)}, bf16[128,512]{0,1:T(8,128)(2,1)}, u32[]{:S(2)}) copy-start(bf16[128,512]{0,1:T(8,128)(2,1)} %copy-done.5) | copy-start | bytes 393220
  166.2 1.0 copy-start.1
  185.1 125.6 %copy-start.10 = (bf16[1,2048,768]{2,1,0:T(8,128)(2,1)S(1)}, bf16[1,2048,768]{2,1,0:T(8,128)(2,1)}, u32[]{:S(2)}) copy-start(bf16[1,2048,768]{2,1,0:T(8,128)(2,1)} %param.34) | copy-start | bytes 9437188
  308.3 2.3 copy-start.3
  331.7 6.5 %copy-start.9 = (f32[1,128,8]{1,2,0:T(8,128)S(1)}, f32[1,128,8]{1,2,0:T(8,128)}, u32[]{:S(2)}) copy-start(f32[1,128,8]{1,2,0:T(8,128)} %param.32) | copy-start | bytes 12292
  331.7 125.4 %all-to-all-start.1 = ((bf16[32,34,2048]{2,1,0:T(8,128)(2,1)}), bf16[32,34,2048]{2,1,0:T(8,128)(2,1)}, u32[]{:S(2)}, u32[]{:S(2)}) async-start(bf16[32,34,2048]{2,1,0:T(8,128)(2,1)} %convolution_convert_fusion), calls=%async_computation.1 | async-start | bytes 10485760 | tf_op jit(solution)/shard_map/all_to_all | solution.py:110
  476.2 6.6 %copy-start.2 = (f32[128,2048]{1,0:T(8,128)S(1)}, f32[128,2048]{1,0:T(8,128)}, u32[]{:S(2)}) copy-start(f32[128,2048]{1,0:T(8,128)} %copy-done.1) | copy-start | bytes 3145732
Sparse Core Ops, SparseCore 0:
  10.1 147.5 all-gather.1
where the time goes:
time: 500 us; the launch traced here: 491 us
  waiting for transfers between devices  184 us (37%)
  blocking collectives  123 us (25%)
  local copies, waits for them, and re-layouts  54.4 us (11%)
  matrix products  45 us (9%)
  starting transfers between devices  34.5 us (7%)
  other arithmetic  31.8 us (6%)
  between operations  14.2 us (3%)
    all_to_all x1, blocking collectives, body(): lax.all_to_all(send_rows, 'exp', split_axis=0, concat_axis=0, tiled=True)  123 us
    all_to_all x1, waiting for transfers between devices, body(): lax.all_to_all(expert_out.reshape(n_exp * local_experts, slots, D), 'exp'...  119 us
    all_gather x1, waiting for transfers between devices, body(): lax.all_gather(out_proj, 'exp', axis=0, tiled=True)  51.9 us
    ppermute x7, starting transfers between devices, shifted(): return lax.ppermute(block, axis, route)  28 us
    another operation x2, other arithmetic  15.6 us
    dot_general x1, matrix products, body(): jnp.einsum('sxcf,xfd->sxcd', activated, w_down, preferred_element_type=jn...  14.6 us
    dot_general x4, matrix products, compute(): jnp.einsum('hgqk,khd->hgqd', weights.astype(jnp.bfloat16), values, prefer...  12.7 us
    ppermute x7, waiting for transfers between devices, shifted(): return lax.ppermute(block, axis, route)  12.6 us
  transfers between devices with their start and end apart: 9, of which 6 were waited for; matrix products, arithmetic and copies ran while one was open for 11% of the time, Pallas kernels for 0%

commit v1 on v0

v1 whole, which is shorter than its diff:
```python
import math

import jax
import jax.numpy as jnp
from jax import lax
from jax.experimental import pallas as pl
from jax.experimental.pallas import tpu as pltpu
from jax.sharding import PartitionSpec as P

D = 2048
QH = 32
KVH = 2
HD = 128
EF = 768
TOP = 8
TOK = 128
EXPERTS = 32
CAP = 34
ROWS = 144
HALF = 64
NZ = 8
NCTX = 8
MESH = pl.DeviceIdType.MESH
BF = jnp.bfloat16
F32 = jnp.float32

A0, A1, B0 = 0, 1, 2
STREAM = ((0, 0), (1, 0), (0, 1))
HOPS = ((4, 3), (3, 4), (4, 3))


class Place:
    def __init__(self):
        ctx, exp = lax.axis_index("ctx"), lax.axis_index("exp")
        self.ctx, self.exp = ctx, exp
        self.xlo, self.y = ctx // 4, ctx % 4
        self.z, self.xhi, self.core = exp // 4, (exp // 2) % 2, exp % 2

    def device(self, xlo, z, xhi, core):
        return {"ctx": xlo * 4 + self.y, "exp": z * 4 + xhi * 2 + core}

    def up(self):
        return self.device(self.xlo, (self.z + 1) % NZ, self.xhi, self.core)

    def down(self):
        return self.device(self.xlo, (self.z + NZ - 1) % NZ, self.xhi, self.core)

    def cross(self):
        return self.device(1 - self.xlo, self.z, 1 - self.xhi, self.core)

    def peer(self):
        return self.device(self.xlo, self.z, self.xhi, 1 - self.core)

    def plane(self, rel):
        return (self.z + rel + NZ) % NZ

    def column(self, col):
        return self.xhi if col == 0 else 1 - self.xhi

    def slot(self, rel, col, core=None):
        core = self.core if core is None else core
        return self.plane(rel) * 4 + self.column(col) * 2 + core


def rels(k):
    return (0,) if k == 0 else ((4,) if k == 4 else (-k, k))


def remote(src, dst, send, recv, device):
    return pltpu.make_async_remote_copy(
        src_ref=src, dst_ref=dst, send_sem=send, recv_sem=recv, device_id=device, device_id_type=MESH
    )


class Gather:
    def __init__(self, at, buf, zs, zr, cs, cr, ps, pr):
        self.at, self.buf = at, buf
        self.zs, self.zr, self.cs, self.cr, self.ps, self.pr = zs, zr, cs, cr, ps, pr
        self.sent = {k: [] for k in range(5)}

    def rows(self, rel, col, half, core=None):
        start = self.at.slot(rel, col, core) * TOK + half * HALF
        return self.buf.at[pl.ds(pl.multiple_of(start, HALF), HALF)]

    def go(self, k, copy):
        copy.start()
        self.sent[k].append(copy)

    def hop(self, stream, direction, k):
        col, half = STREAM[stream]
        if k > HOPS[stream][direction]:
            return
        rel = -(k - 1) if direction == 0 else k - 1
        ref = self.rows(rel, col, half)
        to = self.at.up() if direction == 0 else self.at.down()
        self.go(abs(rel), remote(ref, ref, self.zs.at[stream, direction, k], self.zr.at[stream, direction, k], to))

    def crossing(self, rel, half):
        ref = self.rows(rel, 0, half)
        index = rel % NZ if half == 1 else NZ
        return remote(ref, ref, self.cs.at[index], self.cr.at[index], self.at.cross())

    def crossed(self, rel, half):
        ref = self.rows(rel, 1, half)
        index = rel % NZ if half == 1 else NZ
        remote(ref, ref, self.cs.at[index], self.cr.at[index], self.at.cross()).wait_recv()

    def share(self, rel, col, half):
        ref = self.rows(rel, col, half)
        index = (rel % NZ) * 4 + col * 2 + half
        self.go(abs(rel), remote(ref, ref, self.ps.at[index], self.pr.at[index], self.at.peer()))

    def begin(self):
        self.go(0, self.crossing(0, 0))
        for stream in (A0, B0):
            for direction in (0, 1):
                self.hop(stream, direction, 1)
        self.go(0, self.crossing(0, 1))
        self.share(0, 0, 0)
        self.share(0, 0, 1)

    def begin_column(self):
        self.crossed(0, 0)
        for direction in (0, 1):
            self.hop(A1, direction, 1)
        self.share(0, 1, 0)

    def ring(self, k):
        for stream in (A0, B0, A1):
            col, half = STREAM[stream]
            for direction in (0, 1):
                if k > HOPS[stream][direction]:
                    continue
                rel = -k if direction == 0 else k
                rel = 4 if k == 4 else rel
                ref = self.rows(rel, col, half)
                sem = self.zr.at[stream, direction, k]
                remote(ref, ref, self.zs.at[stream, direction, k], sem, self.at.up()).wait_recv()
                self.hop(stream, direction, k + 1)
                if stream == B0:
                    self.go(k, self.crossing(rel, 1))
                self.share(rel, col, half)

    def column(self, k):
        for rel in rels(k):
            self.crossed(rel, 1)
            self.share(rel, 1, 1)

    def shared(self, k):
        for rel in rels(k):
            for col in (0, 1):
                for half in (0, 1):
                    ref = self.rows(rel, col, half, 1 - self.at.core)
                    index = (rel % NZ) * 4 + col * 2 + half
                    remote(ref, ref, self.ps.at[index], self.pr.at[index], self.at.peer()).wait_recv()

    def settle(self, k):
        for copy in self.sent[k]:
            copy.wait_send()


GATHER_SEMS = [
    pltpu.SemaphoreType.DMA((3, 2, 5)),
    pltpu.SemaphoreType.DMA((3, 2, 5)),
    pltpu.SemaphoreType.DMA((9,)),
    pltpu.SemaphoreType.DMA((9,)),
    pltpu.SemaphoreType.DMA((32,)),
    pltpu.SemaphoreType.DMA((32,)),
]


def attention_kernel(
    hidden_ref, query_ref, kv_ref, proj_ref, gain_ref, gates_ref,
    residual_ref, normed_ref, gates_out,
    weights, heads, kvs, scores, mixed, total,
    zs, zr, cs, cr, ps, pr, ks, kr, gs, gr, own_sem,
):
    at = Place()
    position = at.ctx

    def gate_target(off):
        other = (at.exp + off) % EXPERTS
        other_hi = (other // 2) % 2
        return other, {"ctx": ((at.xlo + at.xhi + other_hi) % 2) * 4 + at.y, "exp": other}

    barrier = pltpu.get_barrier_semaphore()

    def greet(off, carry):
        _, device = gate_target(off)
        pl.semaphore_signal(barrier, inc=1, device_id=device, device_id_type=MESH)
        return carry

    lax.fori_loop(1, EXPERTS, greet, 0)
    for off in range(1, NCTX):
        device = {"ctx": (position + off) % NCTX, "exp": at.exp}
        pl.semaphore_signal(barrier, inc=1, device_id=device, device_id_type=MESH)

    own = pltpu.make_async_copy(proj_ref, weights.at[pl.ds(at.exp * TOK, TOK)], own_sem)
    own.start()
    kvs[pl.ds(pl.multiple_of(position * TOK, TOK), TOK), :] = kv_ref[...]
    for h in range(QH):
        heads[h * TOK : (h + 1) * TOK, :] = query_ref[:, h * HD : (h + 1) * HD]
    gates_out[pl.ds(at.exp, 1)] = gates_ref[pl.ds(at.exp, 1)]
    own.wait()
    pl.semaphore_wait(barrier, EXPERTS - 1 + NCTX - 1)

    gather = Gather(at, weights, zs, zr, cs, cr, ps, pr)
    gather.begin()

    kv_copies = []
    mine = kvs.at[pl.ds(pl.multiple_of(position * TOK, TOK), TOK)]
    for off in (1, 7, 4, 3, 5, 2, 6):
        device = {"ctx": (position + off) % NCTX, "exp": at.exp}
        copy = remote(mine, mine, ks.at[off], kr.at[off], device)
        copy.start()
        kv_copies.append((off, copy))

    def send_gates(off, carry):
        other, device = gate_target(off)
        remote(gates_ref.at[other], gates_out.at[at.exp], gs.at[off], gr.at[off], device).start()
        return carry

    lax.fori_loop(1, EXPERTS, send_gates, 0)
    gather.begin_column()

    for off, _ in kv_copies:
        origin = (position + NCTX - off) % NCTX
        ref = kvs.at[pl.ds(pl.multiple_of(origin * TOK, TOK), TOK)]
        device = {"ctx": origin, "exp": at.exp}
        remote(ref, ref, ks.at[off], kr.at[off], device).wait_recv()

    scale = HD ** (-0.5) * math.log2(math.e)
    last = position // 2
    row_pos = position * TOK + lax.broadcasted_iota(jnp.int32, (2 * TOK, 2 * TOK), 0) % TOK
    key_pos = last * 2 * TOK + lax.broadcasted_iota(jnp.int32, (2 * TOK, 2 * TOK), 1)
    visible = row_pos >= key_pos

    def attend(chunk, carry):
        lane = pl.multiple_of((chunk // 8) * HD, HD)
        q = heads[pl.ds(pl.multiple_of(chunk * 2 * TOK, 2 * TOK), 2 * TOK), :]

        def score(pair):
            keys = kvs[pl.ds(pl.multiple_of(pair * 2 * TOK, 2 * TOK), 2 * TOK), pl.ds(lane, HD)]
            return lax.dot_general(q, keys, (((1,), (1,)), ((), ())), preferred_element_type=F32)

        def first(pair, running):
            s = score(pair)
            scores[pair] = s
            return jnp.maximum(running, jnp.maximum(s[:, :TOK], s[:, TOK:]))

        running = lax.fori_loop(0, last, first, jnp.full((2 * TOK, TOK), -1e30, F32))
        s = jnp.where(visible, score(last), -1e30)
        scores[last] = s
        running = jnp.maximum(running, jnp.maximum(s[:, :TOK], s[:, TOK:]))
        row_max = jnp.max(running, axis=1, keepdims=True)

        def second(pair, state):
            row_sum, acc = state
            weight = jnp.exp2((scores[pair] - row_max) * scale)
            values = kvs[
                pl.ds(pl.multiple_of(pair * 2 * TOK, 2 * TOK), 2 * TOK),
                pl.ds(pl.multiple_of(lane + KVH * HD, HD), HD),
            ]
            acc = acc + jnp.dot(weight.astype(BF), values, preferred_element_type=F32)
            return row_sum + weight[:, :TOK] + weight[:, TOK:], acc

        zero = jnp.zeros((2 * TOK, TOK), F32)
        row_sum, acc = lax.fori_loop(0, last + 1, second, (zero, zero))
        out = (acc / jnp.sum(row_sum, axis=1, keepdims=True)).astype(BF)
        plane, side = chunk // 2, chunk % 2
        for i in range(2):
            columns = pl.ds(pl.multiple_of((side * 2 + i) * HD, HD), HD)
            mixed[plane, :, columns] = out[i * TOK : (i + 1) * TOK]
        return carry

    lax.fori_loop(0, 8, attend, 0)
    gather.column(0)
    gather.ring(1)
    lax.fori_loop(8, 16, attend, 0)

    total[...] = hidden_ref[...].astype(F32)

    def project(rel):
        plane = at.plane(rel)

        def tile(n, carry):
            columns = pl.ds(pl.multiple_of(n * 512, 512), 512)
            part = weights[pl.ds(pl.multiple_of(plane * 512, 512), 512), columns]
            total[:, columns] += jnp.dot(mixed[plane], part, preferred_element_type=F32)
            return carry

        lax.fori_loop(0, 4, tile, 0)

    for k in range(5):
        if k >= 1:
            gather.column(k)
        if k + 1 in (2, 3, 4):
            gather.ring(k + 1)
        gather.shared(k)
        for rel in rels(k):
            project(rel)

    def norm(i, carry):
        rows = pl.ds(pl.multiple_of(i * 16, 16), 16)
        r = total[rows, :]
        inverse = lax.rsqrt(jnp.mean(r * r, axis=-1, keepdims=True) + 1e-06)
        normed_ref[rows, :] = (r * inverse * gain_ref[...].astype(F32)).astype(BF)
        residual_ref[rows, :] = r
        return carry

    lax.fori_loop(0, TOK // 16, norm, 0)

    def take_gates(off, carry):
        other, device = gate_target(off)
        origin = (at.exp + EXPERTS - off) % EXPERTS
        copy = remote(gates_ref.at[other], gates_out.at[origin], gs.at[off], gr.at[off], device)
        copy.wait_send()
        copy.wait_recv()
        return carry

    lax.fori_loop(1, EXPERTS, take_gates, 0)
    for _, copy in kv_copies:
        copy.wait_send()
    for k in range(5):
        gather.settle(k)


def expert_kernel(
    normed_ref, residual_ref, gates_ref, gate_hbm, up_hbm, down_hbm,
    out_ref,
    buf, peer_part, ring_part, cross_part, wg, wu, wd, picked, act, outs,
    zs, zr, cs, cr, ps, pr, rzs, rzr, rcs, rcr, rps, rpr, wsem,
):
    at = Place()
    loads = [
        pltpu.make_async_copy(src, dst, wsem.at[i])
        for i, (src, dst) in enumerate(((gate_hbm, wg), (up_hbm, wu), (down_hbm, wd)))
    ]
    for load in loads:
        load.start()
    barrier = pltpu.get_barrier_semaphore()
    for device in (at.up(), at.down(), at.cross(), at.peer()):
        pl.semaphore_signal(barrier, inc=1, device_id=device, device_id_type=MESH)
    buf[pl.ds(pl.multiple_of(at.exp * TOK, TOK), TOK), :] = normed_ref[...]
    pl.semaphore_wait(barrier, 4)

    gather = Gather(at, buf, zs, zr, cs, cr, ps, pr)
    gather.begin()
    gather.begin_column()

    before = (
        lax.broadcasted_iota(jnp.int32, (TOK, TOK), 0) < lax.broadcasted_iota(jnp.int32, (TOK, TOK), 1)
    ).astype(BF)

    def selection(rel):
        places, gates = [], []
        for s in range(4):
            g = gates_ref[at.plane(rel) * 4 + s]
            named = g > 0.0
            rank = jnp.dot(named.astype(BF), before, preferred_element_type=F32)
            places.append(jnp.where(named, rank + s * CAP, -1.0))
            gates.append(g)
        place = jnp.concatenate(places, axis=1)[0:1]
        gate = jnp.concatenate(gates, axis=1)[0:1]
        number = lax.broadcasted_iota(jnp.int32, (ROWS, 4 * TOK), 0).astype(F32)
        hit = number == place
        gate_rows = jnp.sum(jnp.where(hit, gate, 0.0), axis=1, keepdims=True)
        return hit.astype(BF), gate_rows

    def plane_rows(rel):
        return pl.ds(pl.multiple_of(at.plane(rel) * 512, 512), 512)

    def process(k):
        these = rels(k)
        count = len(these) * ROWS
        chosen = [selection(rel) for rel in these]

        for i, rel in enumerate(these):
            def pick(n, carry):
                columns = pl.ds(pl.multiple_of(n * 512, 512), 512)
                picked[i * ROWS : (i + 1) * ROWS, columns] = jnp.dot(
                    chosen[i][0], buf[plane_rows(rel), columns], preferred_element_type=F32
                ).astype(BF)
                return carry

            lax.fori_loop(0, 4, pick, 0)

        def hidden(n, carry):
            columns = pl.ds(pl.multiple_of(n * 256, 256), 256)
            x = picked[:count, :]
            g = jnp.dot(x, wg[:, columns], preferred_element_type=F32)
            u = jnp.dot(x, wu[:, columns], preferred_element_type=F32)
            act[:count, columns] = (g / (1.0 + jnp.exp(-g)) * u).astype(BF)
            return carry

        lax.fori_loop(0, EF // 256, hidden, 0)
        gate_rows = [c[1] for c in chosen]
        gate_all = gate_rows[0] if len(these) == 1 else jnp.concatenate(gate_rows, axis=0)

        def spread(n, carry):
            columns = pl.ds(pl.multiple_of(n * 512, 512), 512)
            o = jnp.dot(act[:count, :], wd[:, columns], preferred_element_type=F32)
            o = (o * gate_all).astype(BF)
            for i, rel in enumerate(these):
                buf[plane_rows(rel), columns] = lax.dot_general(
                    chosen[i][0], o[i * ROWS : (i + 1) * ROWS], (((0,), (0,)), ((), ())),
                    preferred_element_type=F32,
                ).astype(BF)
            return carry

        lax.fori_loop(0, 4, spread, 0)
        for rel in these:
            for col in (0, 1):
                give_peer(rel, col)

    peer_sent = []

    def peer_copy(rel, col):
        src = buf.at[pl.ds(pl.multiple_of(at.slot(rel, col, 1 - at.core) * TOK, TOK), TOK)]
        dst = peer_part.at[pl.ds(pl.multiple_of((at.plane(rel) * 2 + at.column(col)) * TOK, TOK), TOK)]
        index = (rel % NZ) * 2 + col
        return remote(src, dst, rps.at[index], rpr.at[index], at.peer())

    def give_peer(rel, col):
        copy = peer_copy(rel, col)
        copy.start()
        peer_sent.append(copy)

    for k in range(5):
        if k >= 1:
            gather.column(k)
        else:
            gather.column(0)
        if k + 1 in (1, 2, 3, 4):
            gather.ring(k + 1)
        if k == 0:
            for load in loads:
                load.wait()
        gather.shared(k)
        gather.settle(k)
        process(k)

    back_sent = []

    def mine(rel, col, half):
        return buf.at[pl.ds(pl.multiple_of(at.slot(rel, col) * TOK + half * HALF, HALF), HALF)]

    def from_peer(rel, col, half):
        start = (at.plane(rel) * 2 + at.column(col)) * TOK + half * HALF
        return peer_part.at[pl.ds(pl.multiple_of(start, HALF), HALF)]

    def take_peer(rel):
        for col in (0, 1):
            peer_copy(rel, col).wait_recv()

    def add(target, others):
        def chunk(i, carry):
            rows = pl.ds(pl.multiple_of(i * 16, 16), 16)
            value = target[rows, :].astype(F32)
            for other in others:
                value = value + other[rows, :].astype(F32)
            target[rows, :] = value.astype(BF)
            return carry

        lax.fori_loop(0, HALF // 16, chunk, 0)

    def send_back(copy):
        copy.start()
        back_sent.append(copy)

    def give_cross(rel, half):
        index = rel % NZ if half == 1 else NZ
        send_back(remote(mine(rel, 1, half), cross_part.at[index], rcs.at[index], rcr.at[index], at.cross()))

    def take_cross(rel, half):
        index = rel % NZ if half == 1 else NZ
        part = cross_part.at[index]
        remote(part, part, rcs.at[index], rcr.at[index], at.cross()).wait_recv()
        return part

    def cross_half(rel):
        add(mine(rel, 1, 1), [from_peer(rel, 1, 1)])
        give_cross(rel, 1)

    def ring_slot(stream, direction, k):
        return ring_part.at[(stream * 2 + direction) * 4 + k]

    def take_ring(stream, direction, k):
        part = ring_slot(stream, direction, k)
        remote(
            part, part, rzs.at[stream, direction, k], rzr.at[stream, direction, k], at.up()
        ).wait_recv()
        return part

    def give_ring(stream, direction, k):
        col, half = STREAM[stream]
        if k > HOPS[stream][direction]:
            return
        rel = 4 if k == 4 else (-k if direction == 0 else k)
        others = [from_peer(rel, col, half)]
        if stream == B0:
            others.append(take_cross(rel, 1))
        if k + 1 <= HOPS[stream][direction]:
            others.append(take_ring(stream, direction, k))
        add(mine(rel, col, half), others)
        to = at.down() if direction == 0 else at.up()
        send_back(
            remote(
                mine(rel, col, half),
                ring_slot(stream, direction, k - 1),
                rzs.at[stream, direction, k - 1],
                rzr.at[stream, direction, k - 1],
                to,
            )
        )

    for rel in rels(4):
        take_peer(rel)
        cross_half(rel)
    for k in (4, 3, 2, 1):
        for direction in (0, 1):
            for stream in (A1, A0):
                give_ring(stream, direction, k)
        for rel in rels(k - 1):
            take_peer(rel)
            cross_half(rel)
        for direction in (0, 1):
            give_ring(B0, direction, k)
    add(
        mine(0, 1, 0),
        [from_peer(0, 1, 0), take_ring(A1, 0, 0), take_ring(A1, 1, 0)],
    )
    give_cross(0, 0)

    def finish(half, others):
        def chunk(i, carry):
            rows = pl.ds(pl.multiple_of(i * 16, 16), 16)
            value = mine(0, 0, half)[rows, :].astype(F32)
            for other in others:
                value = value + other[rows, :].astype(F32)
            place = pl.ds(pl.multiple_of(half * HALF + i * 16, 16), 16)
            out_ref[place, :] = (residual_ref[place, :] + value).astype(BF)
            return carry

        lax.fori_loop(0, HALF // 16, chunk, 0)

    finish(1, [from_peer(0, 0, 1), take_cross(0, 1), take_ring(B0, 0, 0), take_ring(B0, 1, 0)])
    finish(0, [from_peer(0, 0, 0), take_ring(A0, 0, 0), take_ring(A0, 1, 0), take_cross(0, 0)])
    for copy in peer_sent + back_sent:
        copy.wait_send()


VMEM = pl.BlockSpec(memory_space=pltpu.VMEM)
ANY = pl.BlockSpec(memory_space=pl.ANY)


def body(
    hidden_in, query, keyval, out_proj, norm_gain, expert_ids, gate_weights, w_gate, w_up, w_down
):
    names = jnp.arange(EXPERTS, dtype=jnp.int32)[:, None, None]
    gates = jnp.sum(
        jnp.where(expert_ids[0].T[None] == names, gate_weights[0].T[None], 0.0), axis=1
    )
    gates = jnp.broadcast_to(gates[:, None, :], (EXPERTS, 8, TOK))

    residual, normed, routed = pl.pallas_call(
        attention_kernel,
        out_shape=(
            jax.ShapeDtypeStruct((TOK, D), F32),
            jax.ShapeDtypeStruct((TOK, D), BF),
            jax.ShapeDtypeStruct((EXPERTS, 8, TOK), F32),
        ),
        in_specs=[VMEM, VMEM, VMEM, ANY, VMEM, VMEM],
        out_specs=(VMEM, VMEM, VMEM),
        scratch_shapes=[
            pltpu.VMEM((QH * HD, D), BF),
            pltpu.VMEM((QH * TOK, HD), BF),
            pltpu.VMEM((NCTX * TOK, 2 * KVH * HD), BF),
            pltpu.VMEM((4, 2 * TOK, 2 * TOK), F32),
            pltpu.VMEM((NZ, TOK, 4 * HD), BF),
            pltpu.VMEM((TOK, D), F32),
            *GATHER_SEMS,
            pltpu.SemaphoreType.DMA((NCTX,)),
            pltpu.SemaphoreType.DMA((NCTX,)),
            pltpu.SemaphoreType.DMA((EXPERTS,)),
            pltpu.SemaphoreType.DMA((EXPERTS,)),
            pltpu.SemaphoreType.DMA(()),
        ],
        compiler_params=pltpu.CompilerParams(
            collective_id=0, has_side_effects=True, vmem_limit_bytes=48 << 20
        ),
        name="attend_project",
    )(hidden_in[0], query[0], keyval[0], out_proj, norm_gain.reshape(1, D), gates)

    result = pl.pallas_call(
        expert_kernel,
        out_shape=jax.ShapeDtypeStruct((TOK, D), BF),
        in_specs=[VMEM, VMEM, VMEM, ANY, ANY, ANY],
        out_specs=VMEM,
        scratch_shapes=[
            pltpu.VMEM((EXPERTS * TOK, D), BF),
            pltpu.VMEM((EXPERTS * TOK // 2, D), BF),
            pltpu.VMEM((24, HALF, D), BF),
            pltpu.VMEM((9, HALF, D), BF),
            pltpu.VMEM((D, EF), BF),
            pltpu.VMEM((D, EF), BF),
            pltpu.VMEM((EF, D), BF),
            pltpu.VMEM((2 * ROWS, D), BF),
            pltpu.VMEM((2 * ROWS, EF), BF),
            pltpu.VMEM((8, 128), BF),
            *GATHER_SEMS,
            pltpu.SemaphoreType.DMA((3, 2, 4)),
            pltpu.SemaphoreType.DMA((3, 2, 4)),
            pltpu.SemaphoreType.DMA((9,)),
            pltpu.SemaphoreType.DMA((9,)),
            pltpu.SemaphoreType.DMA((16,)),
            pltpu.SemaphoreType.DMA((16,)),
            pltpu.SemaphoreType.DMA((3,)),
        ],
        compiler_params=pltpu.CompilerParams(
            collective_id=1, has_side_effects=True, vmem_limit_bytes=58 << 20
        ),
        name="experts",
    )(normed, residual, routed, w_gate[0], w_up[0], w_down[0])
    return result[None]


def solution(mesh):
    in_specs = (
        P("exp", "ctx", None),
        P("exp", "ctx", None),
        P("exp", "ctx", None),
        P("exp", None),
        P(),
        P("exp", "ctx", None),
        P("exp", "ctx", None),
        P("exp", None, None),
        P("exp", None, None),
        P("exp", None, None),
    )
    out_specs = P("exp", "ctx", None)
    return jax.shard_map(body, mesh=mesh, in_specs=in_specs, out_specs=out_specs, check_vma=False)
```

time: 500 us -> 262 us (0.52)
  the two profiles are of different devices: /device:TPU:25 before, /device:TPU:16 now
where the time goes in v1:
time: 262 us
  Pallas kernels  252 us (96%)
  local copies, waits for them, and re-layouts  9.19 us (4%)
    pallas_call x1, Pallas kernels, body(): pl.pallas_call(expert_kernel, out_shape=jax.ShapeDtypeStruct((TOK, D), BF...  158 us
    pallas_call x1, Pallas kernels, body(): pl.pallas_call(attention_kernel, out_shape=(jax.ShapeDtypeStruct((TOK, D)...  93.9 us
    unnamed x15, local copies, waits for them, and re-layouts  8.49 us

profile of v1, /device:TPU:16, one launch (start us, length us, event | category | flops | bytes accessed | tf_op | source)
XLA Modules:
  0.0 262.0 jit_solution(2761535787349239079)
XLA Ops:
  0.0 0.7 reshape.6.gain_ref
  0.7 0.7 fusion.gates_ref
  1.4 0.0 copy-start.1
  1.4 1.2 copy-done.1
  2.7 0.0 copy-start.3
  2.7 1.0 copy-done.3
  3.7 0.0 copy-start.4
  3.7 1.0 copy-done.4
  4.7 0.0 copy-start.6
  4.8 0.9 copy-done.6
  5.7 93.9 %attend_project.1 = (f32[128,2048]{1,0:T(8,128)S(1)}, bf16[128,2048]{1,0:T(8,128)(2,1)S(1)}, f32[32,8,128]{2,1,0:T(8,128)S(1)}) custom-call(bf16[128,2048]{1,0:T(8,128)(2,1)S(1)} %bitcast.14, bf16[128,4096]{1,0:T(8,128)(2,1)S(1)} %bitcast.13, bf16[128,512]{1,0:T(8,128)(2,1)S(1)} %bitcast.15, bf16[128,2048]{1,0:T(8,128)(2,1)S(1)} %copy-done.4, ...), custom_call_target="tpu_custom_call" | custom-call | tf_op jit(solution)/shard_map/attend_project/pallas_call | solution.py:566
  99.6 0.0 copy-start
  99.6 1.0 copy-done
  100.5 0.0 copy-start.2
  100.5 0.8 copy-done.2
  101.3 0.0 copy-start.5
  101.3 0.6 copy-done.5
  102.0 158.2 %experts.1 = bf16[128,2048]{1,0:T(8,128)(2,1)} custom-call(bf16[128,2048]{1,0:T(8,128)(2,1)} %copy-done.2, f32[128,2048]{1,0:T(8,128)} %copy-done, f32[32,8,128]{2,1,0:T(8,128)} %copy-done.5, bf16[2048,768]{1,0:T(8,128)(2,1)} %bitcast.16, bf16[2048,768]{1,0:T(8,128)(2,1)} %bitcast.17, bf16[768,2048]{1,0:T(8,128)(2,1)} %bitcast.18), custom_call_target="tpu_custom_call" | custom-call | tf_op jit(solution)/shard_map/experts/pallas_call | solution.py:595
  260.2 1.9 copy.12
Async XLA Ops:
  1.4 1.2 copy-start.1
  2.7 1.0 copy-start.3
  3.7 1.0 copy-start.4
  4.7 0.9 copy-start.6
  99.6 1.0 copy-start
  100.5 0.8 copy-start.2
  101.3 0.6 copy-start.5

commit v2 on v1

--- a/solution.py
+++ b/solution.py
@@ -1,3 +1,4 @@
+import functools
 import math
 
 import jax
@@ -18,6 +19,8 @@
 CAP = 34
 ROWS = 144
 HALF = 64
+DIRECT = 1024
+QUARTER = 256
 NZ = 8
 NCTX = 8
 MESH = pl.DeviceIdType.MESH
@@ -105,28 +108,29 @@
         index = rel % NZ if half == 1 else NZ
         remote(ref, ref, self.cs.at[index], self.cr.at[index], self.at.cross()).wait_recv()
 
-    def share(self, rel, col, half):
-        ref = self.rows(rel, col, half)
-        index = (rel % NZ) * 4 + col * 2 + half
+    def block(self, rel, col, core=None):
+        return self.buf.at[pl.ds(pl.multiple_of(self.at.slot(rel, col, core) * TOK, TOK), TOK)]
+
+    def share(self, rel, col):
+        ref = self.block(rel, col)
+        index = (rel % NZ) * 2 + col
         self.go(abs(rel), remote(ref, ref, self.ps.at[index], self.pr.at[index], self.at.peer()))
 
     def begin(self):
         self.go(0, self.crossing(0, 0))
-        for stream in (A0, B0):
+        for stream in (B0, A0):
             for direction in (0, 1):
                 self.hop(stream, direction, 1)
         self.go(0, self.crossing(0, 1))
-        self.share(0, 0, 0)
-        self.share(0, 0, 1)
+        self.share(0, 0)
 
     def begin_column(self):
         self.crossed(0, 0)
         for direction in (0, 1):
             self.hop(A1, direction, 1)
-        self.share(0, 1, 0)
 
     def ring(self, k):
-        for stream in (A0, B0, A1):
+        for stream in (B0, A0, A1):
             col, half = STREAM[stream]
             for direction in (0, 1):
                 if k > HOPS[stream][direction]:
@@ -139,20 +143,20 @@
                 self.hop(stream, direction, k + 1)
                 if stream == B0:
                     self.go(k, self.crossing(rel, 1))
-                self.share(rel, col, half)
+                if stream == A0:
+                    self.share(rel, 0)
 
     def column(self, k):
         for rel in rels(k):
             self.crossed(rel, 1)
-            self.share(rel, 1, 1)
+            self.share(rel, 1)
 
     def shared(self, k):
         for rel in rels(k):
             for col in (0, 1):
-                for half in (0, 1):
-                    ref = self.rows(rel, col, half, 1 - self.at.core)
-                    index = (rel % NZ) * 4 + col * 2 + half
-                    remote(ref, ref, self.ps.at[index], self.pr.at[index], self.at.peer()).wait_recv()
+                ref = self.block(rel, col, 1 - self.at.core)
+                index = (rel % NZ) * 2 + col
+                remote(ref, ref, self.ps.at[index], self.pr.at[index], self.at.peer()).wait_recv()
 
     def settle(self, k):
         for copy in self.sent[k]:
@@ -164,19 +168,89 @@
     pltpu.SemaphoreType.DMA((3, 2, 5)),
     pltpu.SemaphoreType.DMA((9,)),
     pltpu.SemaphoreType.DMA((9,)),
-    pltpu.SemaphoreType.DMA((32,)),
-    pltpu.SemaphoreType.DMA((32,)),
+    pltpu.SemaphoreType.DMA((16,)),
+    pltpu.SemaphoreType.DMA((16,)),
 ]
 
 
+class Around:
+    def __init__(self, at, ring, rest, ys, yr, ps, pr):
+        self.at, self.ring, self.rest = at, ring, rest
+        self.ys, self.yr, self.ps, self.pr = ys, yr, ps, pr
+        self.sent = []
+
+    def device(self, off):
+        return {"ctx": self.at.xlo * 4 + (self.at.y + off) % 4, "exp": self.at.exp}
+
+    def rows(self, rel, col, core=None):
+        return pl.ds(pl.multiple_of(self.at.slot(rel, col, core) * TOK, TOK), TOK)
+
+    def copy(self, src, rel, col, off, to):
+        index = (rel % NZ) * 2 + col
+        dst = self.rest.at[off - 1, self.rows(rel, col)]
+        return remote(src, dst, self.ys.at[index, off], self.yr.at[index, off], self.device(to))
+
+    def go(self, copy):
+        copy.start()
+        self.sent.append(copy)
+
+    def give(self, rel, col):
+        src = self.ring.at[self.rows(rel, col), pl.ds(DIRECT, QUARTER)]
+        self.go(self.copy(src, rel, col, 1, 3))
+        self.go(self.copy(src, rel, col, 3, 1))
+
+    def arrived(self, rel, col, off):
+        here = self.rest.at[off - 1, self.rows(rel, col)]
+        self.copy(here, rel, col, off, 1).wait_recv()
+
+    def forward(self, rel, col):
+        self.arrived(rel, col, 1)
+        self.arrived(rel, col, 3)
+        off, to = (3, 1) if col == 0 else (1, 3)
+        self.go(self.copy(self.rest.at[off - 1, self.rows(rel, col)], rel, col, 2, to))
+
+    def share(self, rel, col):
+        if (rel, col) != (0, 0):
+            self.arrived(rel, col, 2)
+        ref = self.rest.at[:, self.rows(rel, col)]
+        index = (rel % NZ) * 2 + col
+        self.go(remote(ref, ref, self.ps.at[index], self.pr.at[index], self.at.peer()))
+
+    def shared(self, k):
+        for rel in rels(k):
+            for col in (0, 1):
+                ref = self.rest.at[:, self.rows(rel, col, 1 - self.at.core)]
+                index = (rel % NZ) * 2 + col
+                remote(ref, ref, self.ps.at[index], self.pr.at[index], self.at.peer()).wait_recv()
+
+    def settle(self):
+        for copy in self.sent:
+            copy.wait_send()
+
+
 def attention_kernel(
-    hidden_ref, query_ref, kv_ref, proj_ref, gain_ref, gates_ref,
+    hidden_hbm, query_hbm, kv_hbm, proj_hbm, gain_ref, gates_ref,
     residual_ref, normed_ref, gates_out,
-    weights, heads, kvs, scores, mixed, total,
-    zs, zr, cs, cr, ps, pr, ks, kr, gs, gr, own_sem,
+    ring, rest, heads, kvs, visible, mixed, total, hidden,
+    zs, zr, cs, cr, ps, pr, ks, kr, gs, gr, ys, yr, yps, ypr, own_sem,
 ):
     at = Place()
     position = at.ctx
+    place = pl.ds(pl.multiple_of(at.exp * TOK, TOK), TOK)
+    loads = [
+        (kv_hbm, kvs.at[pl.ds(pl.multiple_of(position * TOK, TOK), TOK)]),
+        (proj_hbm.at[:, pl.ds(0, DIRECT)], ring.at[place, pl.ds(0, DIRECT)]),
+    ]
+    for off in range(4):
+        columns = pl.ds(pl.multiple_of(DIRECT + (at.y + off) % 4 * QUARTER, QUARTER), QUARTER)
+        to = ring.at[place, pl.ds(DIRECT, QUARTER)] if off == 0 else rest.at[off - 1, place]
+        loads.append((proj_hbm.at[:, columns], to))
+    for h in range(QH):
+        loads.append((query_hbm.at[:, pl.ds(h * HD, HD)], heads.at[pl.ds(h * TOK, TOK)]))
+    loads.append((hidden_hbm, hidden))
+    loads = [pltpu.make_async_copy(src, dst, own_sem.at[i]) for i, (src, dst) in enumerate(loads)]
+    for load in loads:
+        load.start()
 
     def gate_target(off):
         other = (at.exp + off) % EXPERTS
@@ -195,25 +269,28 @@
         device = {"ctx": (position + off) % NCTX, "exp": at.exp}
         pl.semaphore_signal(barrier, inc=1, device_id=device, device_id_type=MESH)
 
-    own = pltpu.make_async_copy(proj_ref, weights.at[pl.ds(at.exp * TOK, TOK)], own_sem)
-    own.start()
-    kvs[pl.ds(pl.multiple_of(position * TOK, TOK), TOK), :] = kv_ref[...]
-    for h in range(QH):
-        heads[h * TOK : (h + 1) * TOK, :] = query_ref[:, h * HD : (h + 1) * HD]
     gates_out[pl.ds(at.exp, 1)] = gates_ref[pl.ds(at.exp, 1)]
-    own.wait()
+
+    @pl.when(position % 2 == 0)
+    def _():
+        kvs[pl.ds(pl.multiple_of((position + 1) * TOK, TOK), TOK), :] = jnp.zeros((TOK, 2 * KVH * HD), BF)
+
+    for load in loads[:6]:
+        load.wait()
     pl.semaphore_wait(barrier, EXPERTS - 1 + NCTX - 1)
 
-    gather = Gather(at, weights, zs, zr, cs, cr, ps, pr)
+    gather = Gather(at, ring, zs, zr, cs, cr, ps, pr)
+    around = Around(at, ring, rest, ys, yr, yps, ypr)
     gather.begin()
 
-    kv_copies = []
     mine = kvs.at[pl.ds(pl.multiple_of(position * TOK, TOK), TOK)]
-    for off in (1, 7, 4, 3, 5, 2, 6):
+
+    def kv_copy(off):
         device = {"ctx": (position + off) % NCTX, "exp": at.exp}
-        copy = remote(mine, mine, ks.at[off], kr.at[off], device)
-        copy.start()
-        kv_copies.append((off, copy))
+        return remote(mine, mine, ks.at[off], kr.at[off], device)
+
+    for off in range(1, NCTX):
+        pl.when(position + off < NCTX)(lambda off=off: kv_copy(off).start())
 
     def send_gates(off, carry):
         other, device = gate_target(off)
@@ -222,50 +299,41 @@
 
     lax.fori_loop(1, EXPERTS, send_gates, 0)
     gather.begin_column()
-
-    for off, _ in kv_copies:
-        origin = (position + NCTX - off) % NCTX
-        ref = kvs.at[pl.ds(pl.multiple_of(origin * TOK, TOK), TOK)]
-        device = {"ctx": origin, "exp": at.exp}
-        remote(ref, ref, ks.at[off], kr.at[off], device).wait_recv()
+    around.share(0, 0)
+    for load in loads[6:]:
+        load.wait()
+
+    def kv_arrived(off):
+        ref = kvs.at[pl.ds(pl.multiple_of((position + NCTX - off) % NCTX * TOK, TOK), TOK)]
+        remote(ref, ref, ks.at[off], kr.at[off], {"ctx": (position + off) % NCTX, "exp": at.exp}).wait_recv()
 
     scale = HD ** (-0.5) * math.log2(math.e)
     last = position // 2
     row_pos = position * TOK + lax.broadcasted_iota(jnp.int32, (2 * TOK, 2 * TOK), 0) % TOK
     key_pos = last * 2 * TOK + lax.broadcasted_iota(jnp.int32, (2 * TOK, 2 * TOK), 1)
-    visible = row_pos >= key_pos
-
-    def attend(chunk, carry):
+    visible[...] = jnp.where(row_pos >= key_pos, 0.0, 1.0)
+
+    def attend(pairs, chunk, carry):
         lane = pl.multiple_of((chunk // 8) * HD, HD)
         q = heads[pl.ds(pl.multiple_of(chunk * 2 * TOK, 2 * TOK), 2 * TOK), :]
-
-        def score(pair):
-            keys = kvs[pl.ds(pl.multiple_of(pair * 2 * TOK, 2 * TOK), 2 * TOK), pl.ds(lane, HD)]
-            return lax.dot_general(q, keys, (((1,), (1,)), ((), ())), preferred_element_type=F32)
-
-        def first(pair, running):
-            s = score(pair)
-            scores[pair] = s
-            return jnp.maximum(running, jnp.maximum(s[:, :TOK], s[:, TOK:]))
-
-        running = lax.fori_loop(0, last, first, jnp.full((2 * TOK, TOK), -1e30, F32))
-        s = jnp.where(visible, score(last), -1e30)
-        scores[last] = s
-        running = jnp.maximum(running, jnp.maximum(s[:, :TOK], s[:, TOK:]))
+        parts, running = [], None
+        for pair in range(pairs):
+            keys = kvs[pair * 2 * TOK : (pair + 1) * 2 * TOK, pl.ds(lane, HD)]
+            s = lax.dot_general(q, keys, (((1,), (1,)), ((), ())), preferred_element_type=F32)
+            if pair == pairs - 1:
+                s = jnp.where(visible[...] == 0.0, s, -1e30)
+            parts.append(s)
+            top = jnp.maximum(s[:, :TOK], s[:, TOK:])
+            running = top if running is None else jnp.maximum(running, top)
         row_max = jnp.max(running, axis=1, keepdims=True)
-
-        def second(pair, state):
-            row_sum, acc = state
-            weight = jnp.exp2((scores[pair] - row_max) * scale)
-            values = kvs[
-                pl.ds(pl.multiple_of(pair * 2 * TOK, 2 * TOK), 2 * TOK),
-                pl.ds(pl.multiple_of(lane + KVH * HD, HD), HD),
-            ]
-            acc = acc + jnp.dot(weight.astype(BF), values, preferred_element_type=F32)
-            return row_sum + weight[:, :TOK] + weight[:, TOK:], acc
-
-        zero = jnp.zeros((2 * TOK, TOK), F32)
-        row_sum, acc = lax.fori_loop(0, last + 1, second, (zero, zero))
+        row_sum, acc = None, None
+        for pair in range(pairs):
+            weight = jnp.exp2((parts[pair] - row_max) * scale)
+            values = kvs[pair * 2 * TOK : (pair + 1) * 2 * TOK, pl.ds(pl.multiple_of(lane + KVH * HD, HD), HD)]
+            part = jnp.dot(weight.astype(BF), values, preferred_element_type=F32)
+            both = weight[:, :TOK] + weight[:, TOK:]
+            acc = part if acc is None else acc + part
+            row_sum = both if row_sum is None else row_sum + both
         out = (acc / jnp.sum(row_sum, axis=1, keepdims=True)).astype(BF)
         plane, side = chunk // 2, chunk % 2
         for i in range(2):
@@ -273,32 +341,91 @@
             mixed[plane, :, columns] = out[i * TOK : (i + 1) * TOK]
         return carry
 
-    lax.fori_loop(0, 8, attend, 0)
+    def some(pairs, first, end):
+        lax.fori_loop(first, end, functools.partial(attend, pairs), 0)
+
+    def attend_some(first, end):
+        for pairs in range(1, NCTX // 2 + 1):
+            pl.when(last == pairs - 1)(
+                lambda pairs=pairs: some(pairs, first, end)
+            )
+
+    def give(k, col):
+        for rel in rels(k):
+            around.give(rel, col)
+
+    def forward(k, col):
+        for rel in rels(k):
+            around.forward(rel, col)
+
+    def share(k):
+        for rel in rels(k):
+            for col in (0, 1):
+                if (rel, col) != (0, 0):
+                    around.share(rel, col)
+
+    def project(k):
+        gather.shared(k)
+        around.shared(k)
+        for rel in rels(k):
+            plane = at.plane(rel)
+            rows = pl.ds(pl.multiple_of(plane * 4 * TOK, 4 * TOK), 4 * TOK)
+
+            def tile(n, carry):
+                columns = pl.ds(pl.multiple_of(n * 512, 512), 512)
+                total[:, columns] += jnp.dot(mixed[plane], ring[rows, columns], preferred_element_type=F32)
+                return carry
+
+            lax.fori_loop(0, DIRECT // 512, tile, 0)
+            for off in range(4):
+                part = ring[rows, DIRECT:] if off == 0 else rest[off - 1, rows, :]
+                columns = pl.ds(pl.multiple_of(DIRECT + (at.y + off) % 4 * QUARTER, QUARTER), QUARTER)
+                total[:, columns] += jnp.dot(mixed[plane], part, preferred_element_type=F32)
+
     gather.column(0)
+    give(0, 1)
     gather.ring(1)
-    lax.fori_loop(8, 16, attend, 0)
-
-    total[...] = hidden_ref[...].astype(F32)
-
-    def project(rel):
-        plane = at.plane(rel)
-
-        def tile(n, carry):
-            columns = pl.ds(pl.multiple_of(n * 512, 512), 512)
-            part = weights[pl.ds(pl.multiple_of(plane * 512, 512), 512), columns]
-            total[:, columns] += jnp.dot(mixed[plane], part, preferred_element_type=F32)
-            return carry
-
-        lax.fori_loop(0, 4, tile, 0)
-
-    for k in range(5):
-        if k >= 1:
-            gather.column(k)
-        if k + 1 in (2, 3, 4):
-            gather.ring(k + 1)
-        gather.shared(k)
-        for rel in rels(k):
-            project(rel)
+    give(1, 0)
+    for off in range(1, NCTX):
+        pl.when(position - off >= 0)(lambda off=off: kv_arrived(off))
+
+    attend_some(0, 5)
+    gather.column(1)
+    give(1, 1)
+    forward(0, 1)
+    gather.ring(2)
+    give(2, 0)
+    forward(1, 0)
+    attend_some(5, 10)
+    gather.column(2)
+    give(2, 1)
+    forward(1, 1)
+    share(0)
+    gather.ring(3)
+    give(3, 0)
+    forward(2, 0)
+    share(1)
+    attend_some(10, 16)
+    total[...] = hidden[...].astype(F32)
+    project(0)
+    gather.column(3)
+    give(3, 1)
+    forward(2, 1)
+    project(1)
+    gather.ring(4)
+    give(4, 0)
+    forward(3, 0)
+    share(2)
+    gather.column(4)
+    give(4, 1)
+    forward(3, 1)
+    project(2)
+    forward(4, 0)
+    share(3)
+    forward(4, 1)
+    project(3)
+    share(4)
+    project(4)
 
     def norm(i, carry):
         rows = pl.ds(pl.multiple_of(i * 16, 16), 16)
@@ -319,29 +446,31 @@
         return carry
 
     lax.fori_loop(1, EXPERTS, take_gates, 0)
-    for _, copy in kv_copies:
-        copy.wait_send()
+    for off in range(1, NCTX):
+        pl.when(position + off < NCTX)(lambda off=off: kv_copy(off).wait_send())
+    around.settle()
     for k in range(5):
         gather.settle(k)
 
 
 def expert_kernel(
-    normed_ref, residual_ref, gates_ref, gate_hbm, up_hbm, down_hbm,
+    normed_hbm, residual_hbm, gates_ref, gate_hbm, up_hbm, down_hbm,
     out_ref,
-    buf, peer_part, ring_part, cross_part, wg, wu, wd, picked, act, outs,
+    buf, peer_part, ring_part, cross_part, wg, wu, wd, picked, act, residual_ref,
     zs, zr, cs, cr, ps, pr, rzs, rzr, rcs, rcr, rps, rpr, wsem,
 ):
     at = Place()
-    loads = [
-        pltpu.make_async_copy(src, dst, wsem.at[i])
-        for i, (src, dst) in enumerate(((gate_hbm, wg), (up_hbm, wu), (down_hbm, wd)))
-    ]
+    place = buf.at[pl.ds(pl.multiple_of(at.exp * TOK, TOK), TOK)]
+    loads = (
+        (normed_hbm, place), (gate_hbm, wg), (up_hbm, wu), (down_hbm, wd), (residual_hbm, residual_ref)
+    )
+    loads = [pltpu.make_async_copy(src, dst, wsem.at[i]) for i, (src, dst) in enumerate(loads)]
     for load in loads:
         load.start()
     barrier = pltpu.get_barrier_semaphore()
     for device in (at.up(), at.down(), at.cross(), at.peer()):
         pl.semaphore_signal(barrier, inc=1, device_id=device, device_id_type=MESH)
-    buf[pl.ds(pl.multiple_of(at.exp * TOK, TOK), TOK), :] = normed_ref[...]
+    loads[0].wait()
     pl.semaphore_wait(barrier, 4)
 
     gather = Gather(at, buf, zs, zr, cs, cr, ps, pr)
@@ -434,7 +563,7 @@
         if k + 1 in (1, 2, 3, 4):
             gather.ring(k + 1)
         if k == 0:
-            for load in loads:
+            for load in loads[1:]:
                 load.wait()
         gather.shared(k)
         gather.settle(k)
@@ -570,21 +699,27 @@
             jax.ShapeDtypeStruct((TOK, D), BF),
             jax.ShapeDtypeStruct((EXPERTS, 8, TOK), F32),
         ),
-        in_specs=[VMEM, VMEM, VMEM, ANY, VMEM, VMEM],
+        in_specs=[ANY, ANY, ANY, ANY, VMEM, VMEM],
         out_specs=(VMEM, VMEM, VMEM),
         scratch_shapes=[
-            pltpu.VMEM((QH * HD, D), BF),
+            pltpu.VMEM((QH * HD, DIRECT + QUARTER), BF),
+            pltpu.VMEM((3, QH * HD, QUARTER), BF),
             pltpu.VMEM((QH * TOK, HD), BF),
             pltpu.VMEM((NCTX * TOK, 2 * KVH * HD), BF),
-            pltpu.VMEM((4, 2 * TOK, 2 * TOK), F32),
+            pltpu.VMEM((2 * TOK, 2 * TOK), F32),
             pltpu.VMEM((NZ, TOK, 4 * HD), BF),
             pltpu.VMEM((TOK, D), F32),
+            pltpu.VMEM((TOK, D), BF),
             *GATHER_SEMS,
             pltpu.SemaphoreType.DMA((NCTX,)),
             pltpu.SemaphoreType.DMA((NCTX,)),
             pltpu.SemaphoreType.DMA((EXPERTS,)),
             pltpu.SemaphoreType.DMA((EXPERTS,)),
-            pltpu.SemaphoreType.DMA(()),
+            pltpu.SemaphoreType.DMA((16, 4)),
+            pltpu.SemaphoreType.DMA((16, 4)),
+            pltpu.SemaphoreType.DMA((16,)),
+            pltpu.SemaphoreType.DMA((16,)),
+            pltpu.SemaphoreType.DMA((QH + 7,)),
         ],
         compiler_params=pltpu.CompilerParams(
             collective_id=0, has_side_effects=True, vmem_limit_bytes=48 << 20
@@ -595,7 +730,7 @@
     result = pl.pallas_call(
         expert_kernel,
         out_shape=jax.ShapeDtypeStruct((TOK, D), BF),
-        in_specs=[VMEM, VMEM, VMEM, ANY, ANY, ANY],
+        in_specs=[ANY, ANY, VMEM, ANY, ANY, ANY],
         out_specs=VMEM,
         scratch_shapes=[
             pltpu.VMEM((EXPERTS * TOK, D), BF),
@@ -607,7 +742,7 @@
             pltpu.VMEM((EF, D), BF),
             pltpu.VMEM((2 * ROWS, D), BF),
             pltpu.VMEM((2 * ROWS, EF), BF),
-            pltpu.VMEM((8, 128), BF),
+            pltpu.VMEM((TOK, D), F32),
             *GATHER_SEMS,
             pltpu.SemaphoreType.DMA((3, 2, 4)),
             pltpu.SemaphoreType.DMA((3, 2, 4)),
@@ -615,7 +750,7 @@
             pltpu.SemaphoreType.DMA((9,)),
             pltpu.SemaphoreType.DMA((16,)),
             pltpu.SemaphoreType.DMA((16,)),
-            pltpu.SemaphoreType.DMA((3,)),
+            pltpu.SemaphoreType.DMA((5,)),
         ],
         compiler_params=pltpu.CompilerParams(
             collective_id=1, has_side_effects=True, vmem_limit_bytes=58 << 20

time: 262 us -> 244 us (0.931)
  Pallas kernels: 252 us -> 234 us
    pallas_call x1, Pallas kernels: 93.9 us -> 73.9 us  [body(): pl.pallas_call(attention_kernel, out_shape=(jax.ShapeDtypeStruct((TOK, D)...]
where the time goes in v2:
time: 244 us
  Pallas kernels  234 us (96%)
  local copies, waits for them, and re-layouts  9.19 us (4%)
    pallas_call x1, Pallas kernels, body(): pl.pallas_call(expert_kernel, out_shape=jax.ShapeDtypeStruct((TOK, D), BF...  160 us
    pallas_call x1, Pallas kernels, body(): pl.pallas_call(attention_kernel, out_shape=(jax.ShapeDtypeStruct((TOK, D)...  73.9 us
    unnamed x15, local copies, waits for them, and re-layouts  8.49 us

profile of v2, /device:TPU:16, one launch (start us, length us, event | category | flops | bytes accessed | tf_op | source)
XLA Modules:
  0.0 243.5 jit_solution(16578552517039460210)
XLA Ops:
  0.0 0.7 reshape.6.gain_ref
  0.7 0.7 fusion.gates_ref
  1.4 0.0 copy-start.1
  1.4 1.2 copy-done.1
  2.7 0.0 copy-start.3
  2.7 1.0 copy-done.3
  3.7 0.0 copy-start.4
  3.7 1.0 copy-done.4
  4.7 0.0 copy-start.6
  4.8 0.9 copy-done.6
  5.7 73.9 %attend_project.1 = (f32[128,2048]{1,0:T(8,128)S(1)}, bf16[128,2048]{1,0:T(8,128)(2,1)S(1)}, f32[32,8,128]{2,1,0:T(8,128)S(1)}) custom-call(bf16[128,2048]{1,0:T(8,128)(2,1)S(1)} %bitcast.14, bf16[128,4096]{1,0:T(8,128)(2,1)S(1)} %bitcast.13, bf16[128,512]{1,0:T(8,128)(2,1)S(1)} %bitcast.15, bf16[128,2048]{1,0:T(8,128)(2,1)S(1)} %copy-done.4, ...), custom_call_target="tpu_custom_call" | custom-call | tf_op jit(solution)/shard_map/attend_project/pallas_call | solution.py:695
  79.6 0.0 copy-start
  79.6 1.0 copy-done
  80.5 0.0 copy-start.2
  80.5 0.8 copy-done.2
  81.3 0.0 copy-start.5
  81.3 0.6 copy-done.5
  82.0 159.7 %experts.1 = bf16[128,2048]{1,0:T(8,128)(2,1)} custom-call(bf16[128,2048]{1,0:T(8,128)(2,1)} %copy-done.2, f32[128,2048]{1,0:T(8,128)} %copy-done, f32[32,8,128]{2,1,0:T(8,128)} %copy-done.5, bf16[2048,768]{1,0:T(8,128)(2,1)} %bitcast.16, bf16[2048,768]{1,0:T(8,128)(2,1)} %bitcast.17, bf16[768,2048]{1,0:T(8,128)(2,1)} %bitcast.18), custom_call_target="tpu_custom_call" | custom-call | tf_op jit(solution)/shard_map/experts/pallas_call | solution.py:730
  241.6 1.9 copy.12
Async XLA Ops:
  1.4 1.2 copy-start.1
  2.7 1.0 copy-start.3
  3.7 1.0 copy-start.4
  4.7 0.9 copy-start.6
  79.6 1.0 copy-start
  80.5 0.8 copy-start.2
  81.3 0.6 copy-start.5
